TPU v7x, 128 devices: a whole 4x4x4 slice. The times are simulated.
128 devices in a mesh: blk: 16 (over x, y), grp: 8 (over z, core).
Axes of the slice: x: 4, y: 4, z: 4, core: 2. Of those that a mesh axis runs over, the one named last changes fastest.
Arguments:
- nodes: bfloat16 [131072, 128], P(('blk', 'grp')), may hold values from -6 to 6
- edges: bfloat16 [524288, 128], P(('blk', 'grp')), may hold values from -6 to 6
- wanted_rows: int32 [2048, 128], P(('blk', 'grp')), may hold values from 0 to 1023, as said below
- sender_slot: int32 [524288], P(('blk', 'grp')), may hold values from 0 to 2047, as said below
- receiver: int32 [524288], P(('blk', 'grp')), may hold values from 0 to 1023
- w_edge_in: bfloat16 [384, 512], replicated, may hold values from -0.3125 to 0.3125
- w_edge_out: bfloat16 [512, 128], replicated, may hold values from -0.25 to 0.25
- w_node_in: bfloat16 [256, 512], replicated, may hold values from -0.375 to 0.375
- w_node_out: bfloat16 [512, 128], replicated, may hold values from -0.25 to 0.25
- node_cot: bfloat16 [131072, 128], P(('blk', 'grp')), may hold values from -6 to 6
- edge_cot: bfloat16 [524288, 128], P(('blk', 'grp')), may hold values from -6 to 6
Outputs:
- new_nodes: bfloat16 [131072, 128], P(('blk', 'grp'))
- new_edges: bfloat16 [524288, 128], P(('blk', 'grp'))
- node_grad: float32 [131072, 128], P(('blk', 'grp'))
- edge_grad: float32 [524288, 128], P(('blk', 'grp'))
- grad_edge_in: float32 [384, 512], replicated
- grad_edge_out: float32 [512, 128], replicated
- grad_node_in: float32 [256, 512], replicated
- grad_node_out: float32 [512, 128], replicated
Inputs may be any that keep to these rules, and one draw needn't show every extreme that they name: `wanted_rows`: row 16 d + p holds 128 distinct local grain rows of the device at blk index p and at device d's grp index. `sender_slot`: on each device, every one of its 2048 slots is named by one or more contacts.
All inputs are finite; a program needn't handle non-finite values.
Results may differ from a plain program's by a relative error of at most 0.015.
Values may be sent and summed in bfloat16 or wider, within the bound.
A program may use at most 128 MiB of HBM per device.

v0:
```python
import functools

import jax
import jax.numpy as jnp
from jax import lax
from jax.experimental import pallas as pl
from jax.experimental.pallas import tpu as pltpu
from jax.sharding import PartitionSpec as P

EPSILON = 1e-05
L = 128
H = 512
NB = 16
NG = 8
GR = 1024
E = 4096
T = 2048
TA = 1024
TB = 1024
EDGE = 4
NODE = 3
F32 = jnp.float32
BF16 = jnp.bfloat16
I16 = jnp.int16
VMEM_LIMIT = 63 * 1024 * 1024
MESH = pl.DeviceIdType.MESH


def mm(a, b):
    return jnp.dot(a, b, preferred_element_type=F32)


def mm_nt(a, b):
    return lax.dot_general(a, b, (((1,), (1,)), ((), ())), preferred_element_type=F32)


def mm_tn(a, b):
    return lax.dot_general(a, b, (((0,), (0,)), ((), ())), preferred_element_type=F32)


def column(rows):
    parts = [
        jnp.transpose(jnp.broadcast_to(rows[i : i + 1, :], (128, 128)))
        for i in range(rows.shape[0])
    ]
    return parts[0] if len(parts) == 1 else jnp.concatenate(parts, axis=0)


def pick(col, width):
    col = col.astype(I16)
    lane = lax.broadcasted_iota(jnp.int32, col.shape, 1).astype(I16)
    one = jnp.ones(col.shape, BF16)
    zero = jnp.zeros(col.shape, BF16)
    return jnp.concatenate(
        [jnp.where(col == lane + I16(128 * j), one, zero) for j in range(width // 128)], axis=1
    )


def spread(rows, width):
    outs = []
    for i in range(rows.shape[0]):
        ids = jnp.broadcast_to(rows[i : i + 1, :], (128, 128)).astype(I16)
        sub = lax.broadcasted_iota(jnp.int32, (128, 128), 0).astype(I16)
        one = jnp.ones((128, 128), BF16)
        zero = jnp.zeros((128, 128), BF16)
        outs.append(
            jnp.concatenate(
                [jnp.where(ids == sub + I16(128 * j), one, zero) for j in range(width // 128)],
                axis=0,
            )
        )
    return outs[0] if len(outs) == 1 else jnp.concatenate(outs, axis=1)


def halves(value, high):
    zero = jnp.zeros_like(value)
    return jnp.concatenate(
        [jnp.where(high, zero, value), jnp.where(high, value, zero)], axis=1
    ).astype(BF16)


def layer_norm(value):
    center = value - jnp.mean(value, axis=-1, keepdims=True)
    inv = lax.rsqrt(jnp.mean(center * center, axis=-1, keepdims=True) + EPSILON)
    return center * inv, inv


def norm_back(upstream, normed, inv):
    first = jnp.mean(upstream, axis=-1, keepdims=True)
    second = jnp.mean(upstream * normed, axis=-1, keepdims=True)
    return (upstream - first - normed * second) * inv


def silu_pair(pre):
    sig = 0.5 * jnp.tanh(0.5 * pre) + 0.5
    hid = pre * sig
    return hid.astype(BF16), sig + hid * (1.0 - sig)


def whole(n):
    return [pl.BlockSpec(memory_space=pltpu.VMEM)] * n


def anywhere(n):
    return [pl.BlockSpec(memory_space=pl.ANY)] * n


def store_block(total, block, value):
    value = value.astype(BF16)
    for half in range(2):
        for i in range(4):
            for j in range(4):
                total[half, 4 * i + j, 16 * block : 16 * block + 16, :] = value[
                    64 * half + 16 * i : 64 * half + 16 * i + 16, 128 * j : 128 * j + 128
                ]


def load_block(out, block, scale):
    lines = []
    for half in range(2):
        for i in range(4):
            lines.append(
                jnp.concatenate(
                    [out[half, 4 * i + j, 16 * block : 16 * block + 16, :] for j in range(4)],
                    axis=1,
                )
            )
    return jnp.concatenate(lines, axis=0).astype(F32) * scale


def distance(k):
    dx, dy = k // 4, k % 4
    return min(dx, 4 - dx) + min(dy, 4 - dy)


FAR_FIRST = sorted(range(1, NB), key=distance, reverse=True)
BATCHES = [[k for k in range(1, NB) if distance(k) in near] for near in ((1,), (2,), (3, 4))]


def ahead(me, k):
    return lax.rem(me // 4 + k // 4, 4) * 4 + lax.rem(lax.rem(me, 4) + k % 4, 4)


def behind(me, k):
    return lax.rem(me // 4 + 4 - k // 4, 4) * 4 + lax.rem(lax.rem(me, 4) + 4 - k % 4, 4)


def remote(src, dst, send, recv, to):
    return pltpu.make_async_remote_copy(
        src_ref=src, dst_ref=dst, send_sem=send, recv_sem=recv, device_id=to, device_id_type=MESH
    )


class Reduce:
    def __init__(self, me, grp, total, out, half_in, mine, piece_in, own, z_in, sems):
        self.me, self.grp = me, grp
        self.core = lax.rem(grp, 2)
        self.zpos = grp // 2
        self.other = (me, grp + 1 - 2 * self.core)
        self.total, self.out, self.half_in, self.mine = total, out, half_in, mine
        self.piece_in, self.own, self.z_in = piece_in, own, z_in
        self.ps, self.pr, self.ls, self.lr = sems

    def pair(self):
        return remote(
            self.total.at[1 - self.core], self.half_in, self.ps.at[0], self.pr.at[0], self.other
        )

    def piece(self, k):
        to = ahead(self.me, k)
        return remote(
            self.mine.at[to],
            self.piece_in.at[self.me],
            self.ls.at[0, k],
            self.lr.at[0, k],
            (to, self.grp),
        )

    def along_z(self, k):
        to = lax.rem(self.grp + 2 * k, NG)
        return remote(
            self.own, self.z_in.at[self.zpos], self.ps.at[1 + k], self.pr.at[1 + k], (self.me, to)
        )

    def spread(self, k):
        to = ahead(self.me, k)
        place = self.out.at[self.core, self.me]
        return remote(place, place, self.ls.at[1, k], self.lr.at[1, k], (to, self.grp))

    def last(self):
        place = self.out.at[self.core]
        return remote(place, place, self.ps.at[1], self.pr.at[1], self.other)

    def start(self):
        self.pair().start()

    def to_line(self):
        self.pair().wait()
        self.mine[...] = (
            self.total[self.core].astype(F32) + self.half_in[...].astype(F32)
        ).astype(BF16)
        for k in FAR_FIRST:
            self.piece(k).start()
        self.piece_in[self.me] = self.mine[self.me]

    def to_z(self):
        for k in range(1, NB):
            self.piece(k).wait()
        acc = self.piece_in[0].astype(F32)
        for q in range(1, NB):
            acc = acc + self.piece_in[q].astype(F32)
        self.own[...] = acc.astype(BF16)
        for k in range(1, 4):
            self.along_z(k).start()
        self.z_in[self.zpos] = self.own[...]

    def to_all(self):
        for k in range(1, 4):
            self.along_z(k).wait()
        acc = self.z_in[0].astype(F32)
        for q in range(1, 4):
            acc = acc + self.z_in[q].astype(F32)
        self.out[self.core, self.me] = acc.astype(BF16)
        for k in FAR_FIRST:
            self.spread(k).start()

    def to_pair(self):
        for k in range(1, NB):
            self.spread(k).wait()
        self.last().start()

    def end(self):
        self.last().wait()


def main_kernel(
    node_scale,
    wanted_h,
    slot_h,
    receiver_h,
    nodes_h,
    edges_h,
    w_ein_h,
    w_eout_h,
    w_nin_h,
    w_nout_h,
    node_cot_h,
    edge_cot_h,
    new_nodes_h,
    new_edges_h,
    edge_grad_h,
    node_grad_h,
    g_nin_h,
    g_nout_h,
    out_e,
    wanted,
    slot,
    receiver,
    nodes,
    g_acc,
    w_ein,
    w_eout,
    w_nin,
    w_nout,
    node_cot,
    edge_cot,
    asked,
    staged,
    rows_in,
    recv_col,
    send_col,
    pick_recv,
    pick_send,
    spread_recv,
    stacked,
    big,
    hidden,
    slope,
    d_out_all,
    slots2,
    nodes2,
    acc_node,
    acc_slot,
    node_part,
    new_nodes,
    new_edges,
    slot_grad,
    slot_in,
    g_nin,
    g_nout,
    total_n,
    out_n,
    half_n,
    mine_n,
    piece_n,
    own_n,
    z_n,
    total_e,
    half_e,
    mine_e,
    piece_e,
    own_e,
    z_e,
    load_sem,
    store_sem,
    s1,
    r1,
    s2,
    r2,
    s3,
    r3,
    n_ps,
    n_pr,
    n_ls,
    n_lr,
    e_ps,
    e_pr,
    e_ls,
    e_lr,
):
    me = lax.axis_index("blk")
    grp = lax.axis_index("grp")
    barrier = pltpu.get_barrier_semaphore()
    greeted = [(ahead(me, k), grp) for k in FAR_FIRST]
    greeted += [(me, lax.rem(grp + 2 * k, NG)) for k in range(1, 4)]
    greeted += [(me, grp + 1 - 2 * lax.rem(grp, 2))]
    for peer in greeted:
        pl.semaphore_signal(barrier, inc=1, device_id=peer, device_id_type=MESH)

    loads = [
        pltpu.make_async_copy(src, dst, load_sem.at[i])
        for i, (src, dst) in enumerate(
            [
                (nodes_h, nodes),
                (receiver_h, receiver),
                (wanted_h, wanted),
                (slot_h, slot),
                (edges_h, stacked.at[:, pl.ds(0, L)]),
                (w_ein_h, w_ein),
                (w_eout_h, w_eout),
                (w_nin_h, w_nin),
                (w_nout_h, w_nout),
                (node_cot_h, node_cot),
                (edge_cot_h, edge_cot),
            ]
        )
    ]
    for copy in loads:
        copy.start()

    red_n = Reduce(
        me, grp, total_n, out_n, half_n, mine_n, piece_n, own_n, z_n, (n_ps, n_pr, n_ls, n_lr)
    )
    red_e = Reduce(
        me, grp, total_e, out_e, half_e, mine_e, piece_e, own_e, z_e, (e_ps, e_pr, e_ls, e_lr)
    )

    def ask(k):
        to = ahead(me, k)
        return remote(wanted.at[to], asked.at[me], s1.at[k], r1.at[k], (to, grp))

    def give(k):
        to = behind(me, k)
        return remote(staged.at[k], rows_in.at[me], s2.at[k], r2.at[k], (to, grp))

    def give_slot(k):
        to = ahead(me, k)
        return remote(slot_grad.at[to], slot_in.at[me], s3.at[k], r3.at[k], (to, grp))

    loads[0].wait()
    loads[1].wait()
    nodes2[:, :L] = nodes[: GR // 2, :]
    nodes2[:, L:] = nodes[GR // 2 :, :]

    def place(t, size):
        return pl.ds(pl.multiple_of(t * size, size), size)

    def recv_hot(t, carry):
        rows = place(t, TA)
        ids = receiver[pl.ds(t * (TA // 128), TA // 128)].reshape(TA // 128, 128)
        col = column(ids)
        recv_col[rows, :] = col
        hot = pick(col & 511, 512)
        pick_recv[rows, :] = hot
        both = mm(hot, nodes2[...])
        stacked[rows, 2 * L :] = jnp.where(col >= 512, both[:, L:], both[:, :L]).astype(BF16)
        return carry

    loads[2].wait()
    loads[3].wait()
    lax.fori_loop(0, E // TA, recv_hot, 0)

    def send_hot(t, carry):
        rows = place(t, TA)
        ids = slot[pl.ds(t * (TA // 128), TA // 128)].reshape(TA // 128, 128)
        col = column(ids)
        send_col[rows, :] = col
        pick_send[rows, :] = pick(col & 1023, 1024)
        return carry

    lax.fori_loop(0, E // TA, send_hot, 0)
    pl.semaphore_wait(barrier, len(greeted))
    for k in FAR_FIRST:
        ask(k).start()
    asked[me] = wanted[me]

    for copy in loads[4:]:
        copy.wait()

    def part_pre(t, carry):
        rows = place(t, T)
        both = jnp.concatenate([stacked[rows, :L], stacked[rows, 2 * L :]], axis=1)
        weight = jnp.concatenate([w_ein[:L, :], w_ein[2 * L :, :]], axis=0)
        big[rows, :] = mm(both, weight)
        return carry

    lax.fori_loop(0, E // T, part_pre, 0)

    def recv_spread(t, carry):
        ids = receiver[pl.ds(t * (TA // 128), TA // 128)].reshape(TA // 128, 128)
        spread_recv[t] = spread(ids & 511, 512)
        return carry

    lax.fori_loop(0, E // TA, recv_spread, 0)
    def look_up(ids):
        col = column(ids)
        both = mm(pick(col & 511, 512), nodes2[...])
        return jnp.where(col >= 512, both[:, L:], both[:, :L]).astype(BF16)

    rows_in[me] = look_up(asked[me])
    for batch in BATCHES:
        for k in batch:
            ask(k).wait_recv()
        found = look_up(jnp.concatenate([asked[behind(me, k)] for k in batch], axis=0))
        for i, k in enumerate(batch):
            staged[k] = found[128 * i : 128 * i + 128]
        for k in reversed(batch):
            give(k).start()

    acc_node[...] = jnp.zeros_like(acc_node)
    acc_slot[...] = jnp.zeros_like(acc_slot)

    for k in range(1, NB):
        ask(k).wait_send()
        give(k).wait()
    for p in range(8):
        slots2[128 * p : 128 * p + 128, :L] = rows_in[p]
        slots2[128 * p : 128 * p + 128, L:] = rows_in[p + 8]

    def cut(step):
        return slice(step * TA, step * TA + TA)

    def gather(rows):
        both = mm(pick_send[rows, :], slots2[...])
        high = send_col[rows, :] >= 1024
        stacked[rows, L : 2 * L] = jnp.where(high, both[:, L:], both[:, :L]).astype(BF16)

    def first(rows):
        pre = big[rows, :] + mm(stacked[rows, L : 2 * L], w_ein[L : 2 * L, :])
        hid, slp = silu_pair(pre)
        hidden[rows, :] = hid
        slope[rows, :] = slp.astype(BF16)

    def second(rows, t):
        norm, inv = layer_norm(mm(hidden[rows, :], w_eout[...]))
        big[rows, :L] = norm
        big[rows, L : 2 * L] = jnp.broadcast_to(inv, (TA, L))
        message = norm.astype(BF16).astype(F32)
        new_edges[rows, :] = (stacked[rows, :L].astype(F32) + message).astype(BF16)
        acc_node[...] += mm(spread_recv[t], halves(message, recv_col[rows, :] >= 512))

    count = E // TA
    for step in range(count + 2):
        if step < count:
            gather(cut(step))
        if 1 <= step <= count:
            first(cut(step - 1))
        if step >= 2:
            second(cut(step - 2), step - 2)
    stores = [pltpu.make_async_copy(new_edges, new_edges_h, store_sem.at[0])]
    stores[0].start()

    inbound = jnp.concatenate([acc_node[:, :L], acc_node[:, L:]], axis=0).astype(BF16)
    node = nodes[...]
    node_input = jnp.concatenate([node, inbound], axis=1)
    hid, slp = silu_pair(mm(node_input, w_nin[...]))
    norm, inv = layer_norm(mm(hid, w_nout[...]))
    new_nodes[...] = (node.astype(F32) + norm).astype(BF16)
    stores.append(pltpu.make_async_copy(new_nodes, new_nodes_h, store_sem.at[1]))
    stores[1].start()
    cot = node_cot[...].astype(F32)
    d_out = norm_back(cot, norm, inv).astype(BF16)
    d_pre = (mm_nt(d_out, w_nout[...]) * slp).astype(BF16)
    d_in = mm_nt(d_pre, w_nin[...])
    node_part[...] = cot + d_in[:, :L]
    d_inbound = d_in[:, L:].astype(BF16)
    nodes2[:, :L] = d_inbound[: GR // 2, :]
    nodes2[:, L:] = d_inbound[GR // 2 :, :]
    store_block(total_n, 2, mm_tn(d_out, hid))
    g_in = mm_tn(node_input, d_pre)
    store_block(total_n, 0, g_in[:128])
    store_block(total_n, 1, g_in[128:])
    acc_node[...] = jnp.zeros_like(acc_node)
    red_n.start()

    def gather_back(rows):
        both = mm(pick_recv[rows, :], nodes2[...])
        big[rows, 3 * L :] = jnp.where(recv_col[rows, :] >= 512, both[:, L:], both[:, :L])

    def back_norm(rows):
        upstream = edge_cot[rows, :].astype(F32) + big[rows, 3 * L :]
        d_out = norm_back(upstream, big[rows, :L], big[rows, L : 2 * L]).astype(BF16)
        d_out_all[rows, :] = d_out
        slope[rows, :] = (mm_nt(d_out, w_eout[...]) * slope[rows, :].astype(F32)).astype(BF16)

    def weight_grads(rows, t):
        g_in = mm_tn(stacked[rows, :], slope[rows, :])
        g_out = mm_tn(d_out_all[rows, :], hidden[rows, :])
        if t > 0:
            g_in = g_in + g_acc[: 3 * L, :]
            g_out = g_out + g_acc[3 * L :, :]
        if t < count - 1:
            g_acc[: 3 * L, :] = g_in
            g_acc[3 * L :, :] = g_out
        else:
            for b in range(3):
                store_block(total_e, b, g_in[128 * b : 128 * b + 128])
            store_block(total_e, 3, g_out)

    for step in range(count + 2):
        if step < count:
            gather_back(cut(step))
        if 1 <= step <= count:
            back_norm(cut(step - 1))
        if step == 2:
            red_n.to_line()
        if step >= 2:
            weight_grads(cut(step - 2), step - 2)
    red_e.start()

    def back_input(t, carry):
        rows = place(t, TB)
        d_in = mm_nt(slope[rows, :], w_ein[...])
        big[rows, 2 * L : 3 * L] = edge_cot[rows, :].astype(F32) + d_in[:, :L]
        send = slot[pl.ds(t * (TB // 128), TB // 128)].reshape(TB // 128, 128)
        acc_slot[...] += mm(
            spread(send & 1023, 1024), halves(d_in[:, L : 2 * L], send_col[rows, :] >= 1024)
        )
        acc_node[...] += mm(spread_recv[t], halves(d_in[:, 2 * L :], recv_col[rows, :] >= 512))

        @pl.when(t == 0)
        def _():
            red_e.to_line()

        @pl.when(t == 2)
        def _():
            red_n.to_z()

        return carry

    lax.fori_loop(0, E // TB, back_input, 0)
    for p in range(8):
        slot_grad[p] = acc_slot[128 * p : 128 * p + 128, :L].astype(BF16)
        slot_grad[p + 8] = acc_slot[128 * p : 128 * p + 128, L:].astype(BF16)
    for k in FAR_FIRST:
        give_slot(k).start()
    slot_in[me] = slot_grad[me]
    stores.append(
        pltpu.make_async_copy(big.at[:, pl.ds(2 * L, L)], edge_grad_h, store_sem.at[2])
    )
    stores[2].start()
    red_n.to_all()
    red_e.to_z()
    node_part[: GR // 2, :] += acc_node[:, :L]
    node_part[GR // 2 :, :] += acc_node[:, L:]
    red_e.to_all()
    red_n.to_pair()
    red_n.end()
    for b in range(2):
        g_nin[128 * b : 128 * b + 128, :] = load_block(out_n, b, node_scale)
    g_nout[...] = jnp.transpose(load_block(out_n, 2, node_scale))
    stores.append(pltpu.make_async_copy(g_nin, g_nin_h, store_sem.at[3]))
    stores.append(pltpu.make_async_copy(g_nout, g_nout_h, store_sem.at[4]))
    stores[3].start()
    stores[4].start()
    for k in range(1, NB):
        give_slot(k).wait()

    def home(q, carry):
        ids = asked[pl.ds(4 * q, 4)].reshape(4, 128)
        values = slot_in[pl.ds(4 * q, 4)].reshape(4 * 128, L)
        node_part[...] += mm(spread(ids, GR), values)
        return carry

    lax.fori_loop(0, NB // 4, home, 0)
    stores.append(pltpu.make_async_copy(node_part, node_grad_h, store_sem.at[5]))
    stores[5].start()
    red_e.to_pair()
    red_e.end()
    for copy in stores:
        copy.wait()


def main(*args):
    sem = pltpu.SemaphoreType.DMA
    vm = pltpu.VMEM

    def reduce_buffers(blocks, with_out):
        rows = 16 * blocks
        out = [vm((2, NB, rows, L), BF16)] * (2 if with_out else 1)
        return out + [
            vm((NB, rows, L), BF16),
            vm((NB, rows, L), BF16),
            vm((NB, rows, L), BF16),
            vm((rows, L), BF16),
            vm((4, rows, L), BF16),
        ]

    return pl.pallas_call(
        functools.partial(main_kernel, float((GR * NB * NG) ** -0.5)),
        name="message_passing",
        out_shape=(
            jax.ShapeDtypeStruct((GR, L), BF16),
            jax.ShapeDtypeStruct((E, L), BF16),
            jax.ShapeDtypeStruct((E, L), F32),
            jax.ShapeDtypeStruct((GR, L), F32),
            jax.ShapeDtypeStruct((2 * L, H), F32),
            jax.ShapeDtypeStruct((H, L), F32),
            jax.ShapeDtypeStruct((2, NB, 16 * EDGE, L), BF16),
        ),
        in_specs=anywhere(11),
        out_specs=anywhere(6) + whole(1),
        scratch_shapes=[
            vm((NB, 1, 128), jnp.int32),
            vm((E // 128, 1, 128), jnp.int32),
            vm((E // 128, 1, 128), jnp.int32),
            vm((GR, L), BF16),
            vm((4 * L, H), F32),
            vm((3 * L, H), BF16),
            vm((H, L), BF16),
            vm((2 * L, H), BF16),
            vm((H, L), BF16),
            vm((GR, L), BF16),
            vm((E, L), BF16),
            vm((NB, 1, 128), jnp.int32),
            vm((NB, 128, L), BF16),
            vm((NB, 128, L), BF16),
            vm((E, L), jnp.int32),
            vm((E, L), jnp.int32),
            vm((E, 512), BF16),
            vm((E, 1024), BF16),
            vm((E // TA, 512, TA), BF16),
            vm((E, 3 * L), BF16),
            vm((E, H), F32),
            vm((E, H), BF16),
            vm((E, H), BF16),
            vm((E, L), BF16),
            vm((GR, 2 * L), BF16),
            vm((GR // 2, 2 * L), BF16),
            vm((GR // 2, 2 * L), F32),
            vm((GR, 2 * L), F32),
            vm((GR, L), F32),
            vm((GR, L), BF16),
            vm((E, L), BF16),
            vm((NB, 128, L), BF16),
            vm((NB, 128, L), BF16),
            vm((2 * L, H), F32),
            vm((H, L), F32),
        ]
        + reduce_buffers(NODE, True)
        + reduce_buffers(EDGE, False)
        + [sem((11,)), sem((6,))]
        + [sem((NB,))] * 6
        + [sem((5,)), sem((5,)), sem((2, NB)), sem((2, NB))] * 2,
        compiler_params=pltpu.CompilerParams(
            collective_id=0, has_side_effects=True, vmem_limit_bytes=VMEM_LIMIT
        ),
    )(*args)


def finish_kernel(edge_scale, *refs):
    count = 7
    sources, targets = refs[:count], refs[count : 2 * count - 1]
    g_ein_h, g_eout_h = refs[2 * count - 1 : 2 * count + 1]
    held = refs[2 * count + 1 : 3 * count + 1]
    g_ein, g_eout, load_sem, store_sem = refs[3 * count + 1 :]
    loads = [
        pltpu.make_async_copy(sources[i], held[i], load_sem.at[i]) for i in range(count)
    ]
    stores = [
        pltpu.make_async_copy(held[i + 1], targets[i], store_sem.at[i]) for i in range(count - 1)
    ]
    stores += [
        pltpu.make_async_copy(g_ein, g_ein_h, store_sem.at[count - 1]),
        pltpu.make_async_copy(g_eout, g_eout_h, store_sem.at[count]),
    ]
    for copy in loads:
        copy.start()
    out = held[0]
    loads[0].wait()
    for b in range(3):
        g_ein[128 * b : 128 * b + 128, :] = load_block(out, b, edge_scale)
    stores[-2].start()
    g_eout[...] = jnp.transpose(load_block(out, 3, edge_scale))
    stores[-1].start()
    for load, store in zip(loads[1:], stores):
        load.wait()
        store.start()
    for copy in stores:
        copy.wait()


def finish(out, *arrays):
    grads = (
        jax.ShapeDtypeStruct((3 * L, H), F32),
        jax.ShapeDtypeStruct((H, L), F32),
    )
    return pl.pallas_call(
        functools.partial(finish_kernel, float((E * NB * NG) ** -0.5)),
        name="finish",
        out_shape=tuple(jax.ShapeDtypeStruct(a.shape, a.dtype) for a in arrays) + grads,
        in_specs=anywhere(7),
        out_specs=anywhere(8),
        scratch_shapes=[pltpu.VMEM(a.shape, a.dtype) for a in (out,) + arrays + grads]
        + [pltpu.SemaphoreType.DMA((7,)), pltpu.SemaphoreType.DMA((8,))],
        compiler_params=pltpu.CompilerParams(vmem_limit_bytes=VMEM_LIMIT),
    )(out, *arrays)


def on_device(
    nodes,
    edges,
    wanted_rows,
    sender_slot,
    receiver,
    w_edge_in,
    w_edge_out,
    w_node_in,
    w_node_out,
    node_cot,
    edge_cot,
):
    *arrays, out = main(
        wanted_rows.reshape(NB, 1, 128),
        sender_slot.reshape(E // 128, 1, 128),
        receiver.reshape(E // 128, 1, 128),
        nodes,
        edges,
        w_edge_in,
        w_edge_out,
        w_node_in,
        w_node_out,
        node_cot,
        edge_cot,
    )
    new_nodes, new_edges, edge_grad, node_grad, g_nin, g_nout, g_ein, g_eout = finish(out, *arrays)
    return new_nodes, new_edges, node_grad, edge_grad, g_ein, g_eout, g_nin, g_nout


def solution(mesh):
    split = P(("blk", "grp"), None)
    line = P(("blk", "grp"))
    return jax.shard_map(
        on_device,
        mesh=mesh,
        in_specs=(split, split, split, line, line, P(), P(), P(), P(), split, split),
        out_specs=(split, split, split, split, P(), P(), P(), P()),
        check_vma=False,
    )
```

profile of v0, /device:TPU:1, one launch (start us, length us, event | category | flops | bytes accessed | tf_op | source)
XLA Modules:
  0.0 65.9 jit_solution(10433000716631724234)
XLA Ops:
  0.6 60.8 %message_passing.1 = (bf16[1024,128]{1,0:T(8,128)(2,1)}, bf16[4096,128]{1,0:T(8,128)(2,1)}, f32[4096,128]{1,0:T(8,128)}, f32[1024,128]{1,0:T(8,128)}, f32[256,51...) custom-call(s32[16,1,128]{2,1,0:T(1,128)} %bitcast.5, s32[32,1,128]{2,1,0:T(1,128)} %bitcast.3, ...), custom_call_target="tpu_custom_call" | custom-call | tf_op jit(solution)/shard_map/message_passing/pallas_call | solution.py:619
  61.5 4.2 %finish.1 = (bf16[1024,128]{1,0:T(8,128)(2,1)}, bf16[4096,128]{1,0:T(8,128)(2,1)}, f32[4096,128]{1,0:T(8,128)}, f32[1024,128]{1,0:T(8,128)}, f32[256,512]{1,0:T(...) custom-call(bf16[2,16,64,128]{3,2,1,0:T(8,128)(2,1)} %get-tuple-element.23.refs_0_, ...), custom_call_target="tpu_custom_call" | custom-call | tf_op jit(solution)/shard_map/finish/pallas_call | solution.py:718
where the time goes:
time: 66 us; the launch traced here: 65.9 us
  Pallas kernels  65.1 us (99%)
  between operations  0.81 us (1%)
    pallas_call x1, Pallas kernels, main(): pl.pallas_call(functools.partial(main_kernel, float((GR * NB * NG) ** (-0...  60.8 us
    pallas_call x1, Pallas kernels, finish(): pl.pallas_call(functools.partial(finish_kernel, float((E * NB * NG) ** (-...  4.23 us

commit v1 on v0

--- a/solution.py
+++ b/solution.py
@@ -152,12 +152,13 @@
 
 
 class Reduce:
-    def __init__(self, me, grp, total, out, half_in, mine, piece_in, own, z_in, sems):
+    def __init__(self, me, grp, total, out, target, half_in, mine, piece_in, own, z_in, sems):
         self.me, self.grp = me, grp
         self.core = lax.rem(grp, 2)
         self.zpos = grp // 2
         self.other = (me, grp + 1 - 2 * self.core)
-        self.total, self.out, self.half_in, self.mine = total, out, half_in, mine
+        self.total, self.out, self.target = total, out, target
+        self.half_in, self.mine = half_in, mine
         self.piece_in, self.own, self.z_in = piece_in, own, z_in
         self.ps, self.pr, self.ls, self.lr = sems
 
@@ -188,8 +189,13 @@
         return remote(place, place, self.ls.at[1, k], self.lr.at[1, k], (to, self.grp))
 
     def last(self):
-        place = self.out.at[self.core]
-        return remote(place, place, self.ps.at[1], self.pr.at[1], self.other)
+        return remote(
+            self.out.at[self.core],
+            self.target.at[self.core],
+            self.ps.at[1],
+            self.pr.at[1],
+            self.other,
+        )
 
     def start(self):
         self.pair().start()
@@ -252,12 +258,11 @@
     node_grad_h,
     g_nin_h,
     g_nout_h,
-    out_e,
+    out_h,
     wanted,
     slot,
     receiver,
     nodes,
-    g_acc,
     w_ein,
     w_eout,
     w_nin,
@@ -296,6 +301,7 @@
     own_n,
     z_n,
     total_e,
+    out_e,
     half_e,
     mine_e,
     piece_e,
@@ -349,10 +355,30 @@
         copy.start()
 
     red_n = Reduce(
-        me, grp, total_n, out_n, half_n, mine_n, piece_n, own_n, z_n, (n_ps, n_pr, n_ls, n_lr)
+        me,
+        grp,
+        total_n,
+        out_n,
+        out_n,
+        half_n,
+        mine_n,
+        piece_n,
+        own_n,
+        z_n,
+        (n_ps, n_pr, n_ls, n_lr),
     )
     red_e = Reduce(
-        me, grp, total_e, out_e, half_e, mine_e, piece_e, own_e, z_e, (e_ps, e_pr, e_ls, e_lr)
+        me,
+        grp,
+        total_e,
+        out_e,
+        out_h,
+        half_e,
+        mine_e,
+        piece_e,
+        own_e,
+        z_e,
+        (e_ps, e_pr, e_ls, e_lr),
     )
 
     def ask(k):
@@ -379,7 +405,7 @@
         rows = place(t, TA)
         ids = receiver[pl.ds(t * (TA // 128), TA // 128)].reshape(TA // 128, 128)
         col = column(ids)
-        recv_col[rows, :] = col
+        recv_col[rows, :] = col.astype(I16)
         hot = pick(col & 511, 512)
         pick_recv[rows, :] = hot
         both = mm(hot, nodes2[...])
@@ -394,7 +420,7 @@
         rows = place(t, TA)
         ids = slot[pl.ds(t * (TA // 128), TA // 128)].reshape(TA // 128, 128)
         col = column(ids)
-        send_col[rows, :] = col
+        send_col[rows, :] = col.astype(I16)
         pick_send[rows, :] = pick(col & 1023, 1024)
         return carry
 
@@ -437,8 +463,6 @@
         for k in reversed(batch):
             give(k).start()
 
-    acc_node[...] = jnp.zeros_like(acc_node)
-    acc_slot[...] = jnp.zeros_like(acc_slot)
 
     for k in range(1, NB):
         ask(k).wait_send()
@@ -452,7 +476,7 @@
 
     def gather(rows):
         both = mm(pick_send[rows, :], slots2[...])
-        high = send_col[rows, :] >= 1024
+        high = send_col[rows, :].astype(jnp.int32) >= 1024
         stacked[rows, L : 2 * L] = jnp.where(high, both[:, L:], both[:, :L]).astype(BF16)
 
     def first(rows):
@@ -467,7 +491,8 @@
         big[rows, L : 2 * L] = jnp.broadcast_to(inv, (TA, L))
         message = norm.astype(BF16).astype(F32)
         new_edges[rows, :] = (stacked[rows, :L].astype(F32) + message).astype(BF16)
-        acc_node[...] += mm(spread_recv[t], halves(message, recv_col[rows, :] >= 512))
+        to_node = mm(spread_recv[t], halves(message, recv_col[rows, :].astype(jnp.int32) >= 512))
+        acc_node[...] = to_node if t == 0 else acc_node[...] + to_node
 
     count = E // TA
     for step in range(count + 2):
@@ -492,20 +517,21 @@
     d_out = norm_back(cot, norm, inv).astype(BF16)
     d_pre = (mm_nt(d_out, w_nout[...]) * slp).astype(BF16)
     d_in = mm_nt(d_pre, w_nin[...])
-    node_part[...] = cot + d_in[:, :L]
     d_inbound = d_in[:, L:].astype(BF16)
     nodes2[:, :L] = d_inbound[: GR // 2, :]
     nodes2[:, L:] = d_inbound[GR // 2 :, :]
-    store_block(total_n, 2, mm_tn(d_out, hid))
-    g_in = mm_tn(node_input, d_pre)
-    store_block(total_n, 0, g_in[:128])
-    store_block(total_n, 1, g_in[128:])
-    acc_node[...] = jnp.zeros_like(acc_node)
-    red_n.start()
+
+    def node_grads():
+        node_part[...] = cot + d_in[:, :L]
+        store_block(total_n, 2, mm_tn(d_out, hid))
+        g_in = mm_tn(node_input, d_pre)
+        store_block(total_n, 0, g_in[:128])
+        store_block(total_n, 1, g_in[128:])
+
 
     def gather_back(rows):
         both = mm(pick_recv[rows, :], nodes2[...])
-        big[rows, 3 * L :] = jnp.where(recv_col[rows, :] >= 512, both[:, L:], both[:, :L])
+        big[rows, 3 * L :] = jnp.where(recv_col[rows, :].astype(jnp.int32) >= 512, both[:, L:], both[:, :L])
 
     def back_norm(rows):
         upstream = edge_cot[rows, :].astype(F32) + big[rows, 3 * L :]
@@ -517,11 +543,13 @@
         g_in = mm_tn(stacked[rows, :], slope[rows, :])
         g_out = mm_tn(d_out_all[rows, :], hidden[rows, :])
         if t > 0:
-            g_in = g_in + g_acc[: 3 * L, :]
-            g_out = g_out + g_acc[3 * L :, :]
+            g_in = g_in + jnp.concatenate([acc_slot[:384, :], acc_slot[384:768, :]], axis=1)
+            g_out = g_out + jnp.concatenate([acc_slot[768:896, :], acc_slot[896:, :]], axis=1)
         if t < count - 1:
-            g_acc[: 3 * L, :] = g_in
-            g_acc[3 * L :, :] = g_out
+            acc_slot[:384, :] = g_in[:, : H // 2]
+            acc_slot[384:768, :] = g_in[:, H // 2 :]
+            acc_slot[768:896, :] = g_out[:, : H // 2]
+            acc_slot[896:, :] = g_out[:, H // 2 :]
         else:
             for b in range(3):
                 store_block(total_e, b, g_in[128 * b : 128 * b + 128])
@@ -530,6 +558,9 @@
     for step in range(count + 2):
         if step < count:
             gather_back(cut(step))
+        if step == 0:
+            node_grads()
+            red_n.start()
         if 1 <= step <= count:
             back_norm(cut(step - 1))
         if step == 2:
@@ -538,27 +569,26 @@
             weight_grads(cut(step - 2), step - 2)
     red_e.start()
 
-    def back_input(t, carry):
-        rows = place(t, TB)
+    def back_input(rows):
         d_in = mm_nt(slope[rows, :], w_ein[...])
         big[rows, 2 * L : 3 * L] = edge_cot[rows, :].astype(F32) + d_in[:, :L]
-        send = slot[pl.ds(t * (TB // 128), TB // 128)].reshape(TB // 128, 128)
-        acc_slot[...] += mm(
-            spread(send & 1023, 1024), halves(d_in[:, L : 2 * L], send_col[rows, :] >= 1024)
-        )
-        acc_node[...] += mm(spread_recv[t], halves(d_in[:, 2 * L :], recv_col[rows, :] >= 512))
-
-        @pl.when(t == 0)
-        def _():
+        pick_send[rows, : 2 * L] = halves(d_in[:, L : 2 * L], send_col[rows, :].astype(jnp.int32) >= 1024)
+        pick_send[rows, 2 * L : 4 * L] = halves(d_in[:, 2 * L :], recv_col[rows, :].astype(jnp.int32) >= 512)
+
+    def scatter(rows, t):
+        send = slot[TA // 128 * t : TA // 128 * (t + 1)].reshape(TA // 128, 128)
+        to_slot = mm(spread(send & 1023, 1024), pick_send[rows, : 2 * L])
+        to_node = mm(spread_recv[t], pick_send[rows, 2 * L : 4 * L])
+        acc_slot[...] = to_slot if t == 0 else acc_slot[...] + to_slot
+        acc_node[...] = to_node if t == 0 else acc_node[...] + to_node
+
+    for step in range(count + 1):
+        if step < count:
+            back_input(cut(step))
+        if step == 0:
             red_e.to_line()
-
-        @pl.when(t == 2)
-        def _():
-            red_n.to_z()
-
-        return carry
-
-    lax.fori_loop(0, E // TB, back_input, 0)
+        if step >= 1:
+            scatter(cut(step - 1), step - 1)
     for p in range(8):
         slot_grad[p] = acc_slot[128 * p : 128 * p + 128, :L].astype(BF16)
         slot_grad[p + 8] = acc_slot[128 * p : 128 * p + 128, L:].astype(BF16)
@@ -569,11 +599,24 @@
         pltpu.make_async_copy(big.at[:, pl.ds(2 * L, L)], edge_grad_h, store_sem.at[2])
     )
     stores[2].start()
-    red_n.to_all()
-    red_e.to_z()
     node_part[: GR // 2, :] += acc_node[:, :L]
     node_part[GR // 2 :, :] += acc_node[:, L:]
+    red_n.to_z()
+    red_e.to_z()
+    red_n.to_all()
     red_e.to_all()
+    for k in range(1, NB):
+        give_slot(k).wait()
+
+    def home(q, carry):
+        ids = asked[pl.ds(4 * q, 4)].reshape(4, 128)
+        values = slot_in[pl.ds(4 * q, 4)].reshape(4 * 128, L)
+        node_part[...] += mm(spread(ids, GR), values)
+        return carry
+
+    lax.fori_loop(0, NB // 4, home, 0)
+    stores.append(pltpu.make_async_copy(node_part, node_grad_h, store_sem.at[5]))
+    stores[3].start()
     red_n.to_pair()
     red_n.end()
     for b in range(2):
@@ -581,21 +624,12 @@
     g_nout[...] = jnp.transpose(load_block(out_n, 2, node_scale))
     stores.append(pltpu.make_async_copy(g_nin, g_nin_h, store_sem.at[3]))
     stores.append(pltpu.make_async_copy(g_nout, g_nout_h, store_sem.at[4]))
-    stores[3].start()
     stores[4].start()
-    for k in range(1, NB):
-        give_slot(k).wait()
-
-    def home(q, carry):
-        ids = asked[pl.ds(4 * q, 4)].reshape(4, 128)
-        values = slot_in[pl.ds(4 * q, 4)].reshape(4 * 128, L)
-        node_part[...] += mm(spread(ids, GR), values)
-        return carry
-
-    lax.fori_loop(0, NB // 4, home, 0)
-    stores.append(pltpu.make_async_copy(node_part, node_grad_h, store_sem.at[5]))
     stores[5].start()
     red_e.to_pair()
+    core = lax.rem(grp, 2)
+    stores.append(pltpu.make_async_copy(out_e.at[core], out_h.at[core], store_sem.at[6]))
+    stores[6].start()
     red_e.end()
     for copy in stores:
         copy.wait()
@@ -605,10 +639,9 @@
     sem = pltpu.SemaphoreType.DMA
     vm = pltpu.VMEM
 
-    def reduce_buffers(blocks, with_out):
+    def reduce_buffers(blocks):
         rows = 16 * blocks
-        out = [vm((2, NB, rows, L), BF16)] * (2 if with_out else 1)
-        return out + [
+        return [vm((2, NB, rows, L), BF16)] * 2 + [
             vm((NB, rows, L), BF16),
             vm((NB, rows, L), BF16),
             vm((NB, rows, L), BF16),
@@ -629,13 +662,12 @@
             jax.ShapeDtypeStruct((2, NB, 16 * EDGE, L), BF16),
         ),
         in_specs=anywhere(11),
-        out_specs=anywhere(6) + whole(1),
+        out_specs=anywhere(7),
         scratch_shapes=[
             vm((NB, 1, 128), jnp.int32),
             vm((E // 128, 1, 128), jnp.int32),
             vm((E // 128, 1, 128), jnp.int32),
             vm((GR, L), BF16),
-            vm((4 * L, H), F32),
             vm((3 * L, H), BF16),
             vm((H, L), BF16),
             vm((2 * L, H), BF16),
@@ -645,8 +677,8 @@
             vm((NB, 1, 128), jnp.int32),
             vm((NB, 128, L), BF16),
             vm((NB, 128, L), BF16),
-            vm((E, L), jnp.int32),
-            vm((E, L), jnp.int32),
+            vm((E, L), I16),
+            vm((E, L), I16),
             vm((E, 512), BF16),
             vm((E, 1024), BF16),
             vm((E // TA, 512, TA), BF16),
@@ -667,9 +699,9 @@
             vm((2 * L, H), F32),
             vm((H, L), F32),
         ]
-        + reduce_buffers(NODE, True)
-        + reduce_buffers(EDGE, False)
-        + [sem((11,)), sem((6,))]
+        + reduce_buffers(NODE)
+        + reduce_buffers(EDGE)
+        + [sem((11,)), sem((7,))]
         + [sem((NB,))] * 6
         + [sem((5,)), sem((5,)), sem((2, NB)), sem((2, NB))] * 2,
         compiler_params=pltpu.CompilerParams(

time: 66 us -> 65.2 us (0.988)
  Pallas kernels: 65.1 us -> 64.3 us
    pallas_call x1, Pallas kernels: 60.8 us -> 60.1 us  [main(): pl.pallas_call(functools.partial(main_kernel, float((GR * NB * NG) ** (-0...]
where the time goes in v1:
time: 65.2 us; the launch traced here: 65.1 us
  Pallas kernels  64.3 us (99%)
  between operations  0.81 us (1%)
    pallas_call x1, Pallas kernels, main(): pl.pallas_call(functools.partial(main_kernel, float((GR * NB * NG) ** (-0...  60.1 us
    pallas_call x1, Pallas kernels, finish(): pl.pallas_call(functools.partial(finish_kernel, float((E * NB * NG) ** (-...  4.23 us

profile of v1, /device:TPU:1, one launch (start us, length us, event | category | flops | bytes accessed | tf_op | source)
XLA Modules:
  0.0 65.1 jit_solution(5385832875890107642)
XLA Ops:
  0.6 60.1 %message_passing.1 = (bf16[1024,128]{1,0:T(8,128)(2,1)}, bf16[4096,128]{1,0:T(8,128)(2,1)}, f32[4096,128]{1,0:T(8,128)}, f32[1024,128]{1,0:T(8,128)}, f32[256,51...) custom-call(s32[16,1,128]{2,1,0:T(1,128)} %bitcast.5, s32[32,1,128]{2,1,0:T(1,128)} %bitcast.3, ...), custom_call_target="tpu_custom_call" | custom-call | tf_op jit(solution)/shard_map/message_passing/pallas_call | solution.py:652
  60.7 4.2 %finish.1 = (bf16[1024,128]{1,0:T(8,128)(2,1)}, bf16[4096,128]{1,0:T(8,128)(2,1)}, f32[4096,128]{1,0:T(8,128)}, f32[1024,128]{1,0:T(8,128)}, f32[256,512]{1,0:T(...) custom-call(bf16[2,16,64,128]{3,2,1,0:T(8,128)(2,1)} %get-tuple-element.23.refs_0_, ...), custom_call_target="tpu_custom_call" | custom-call | tf_op jit(solution)/shard_map/finish/pallas_call | solution.py:750

commit v2 on v1

--- a/solution.py
+++ b/solution.py
@@ -240,7 +240,6 @@
 
 
 def main_kernel(
-    node_scale,
     wanted_h,
     slot_h,
     receiver_h,
@@ -256,8 +255,7 @@
     new_edges_h,
     edge_grad_h,
     node_grad_h,
-    g_nin_h,
-    g_nout_h,
+    out_nh,
     out_h,
     wanted,
     slot,
@@ -291,8 +289,6 @@
     new_edges,
     slot_grad,
     slot_in,
-    g_nin,
-    g_nout,
     total_n,
     out_n,
     half_n,
@@ -359,7 +355,7 @@
         grp,
         total_n,
         out_n,
-        out_n,
+        out_nh,
         half_n,
         mine_n,
         piece_n,
@@ -556,6 +552,8 @@
             store_block(total_e, 3, g_out)
 
     for step in range(count + 2):
+        if step == 2:
+            red_n.to_line()
         if step < count:
             gather_back(cut(step))
         if step == 0:
@@ -563,11 +561,10 @@
             red_n.start()
         if 1 <= step <= count:
             back_norm(cut(step - 1))
-        if step == 2:
-            red_n.to_line()
         if step >= 2:
             weight_grads(cut(step - 2), step - 2)
     red_e.start()
+    red_e.to_line()
 
     def back_input(rows):
         d_in = mm_nt(slope[rows, :], w_ein[...])
@@ -585,10 +582,10 @@
     for step in range(count + 1):
         if step < count:
             back_input(cut(step))
-        if step == 0:
-            red_e.to_line()
         if step >= 1:
             scatter(cut(step - 1), step - 1)
+        if step == 2:
+            red_n.to_z()
     for p in range(8):
         slot_grad[p] = acc_slot[128 * p : 128 * p + 128, :L].astype(BF16)
         slot_grad[p + 8] = acc_slot[128 * p : 128 * p + 128, L:].astype(BF16)
@@ -599,11 +596,10 @@
         pltpu.make_async_copy(big.at[:, pl.ds(2 * L, L)], edge_grad_h, store_sem.at[2])
     )
     stores[2].start()
+    red_n.to_all()
     node_part[: GR // 2, :] += acc_node[:, :L]
     node_part[GR // 2 :, :] += acc_node[:, L:]
-    red_n.to_z()
     red_e.to_z()
-    red_n.to_all()
     red_e.to_all()
     for k in range(1, NB):
         give_slot(k).wait()
@@ -617,19 +613,14 @@
     lax.fori_loop(0, NB // 4, home, 0)
     stores.append(pltpu.make_async_copy(node_part, node_grad_h, store_sem.at[5]))
     stores[3].start()
+    core = lax.rem(grp, 2)
     red_n.to_pair()
+    stores.append(pltpu.make_async_copy(out_n.at[core], out_nh.at[core], store_sem.at[3]))
+    stores[4].start()
+    red_e.to_pair()
+    stores.append(pltpu.make_async_copy(out_e.at[core], out_h.at[core], store_sem.at[4]))
+    stores[5].start()
     red_n.end()
-    for b in range(2):
-        g_nin[128 * b : 128 * b + 128, :] = load_block(out_n, b, node_scale)
-    g_nout[...] = jnp.transpose(load_block(out_n, 2, node_scale))
-    stores.append(pltpu.make_async_copy(g_nin, g_nin_h, store_sem.at[3]))
-    stores.append(pltpu.make_async_copy(g_nout, g_nout_h, store_sem.at[4]))
-    stores[4].start()
-    stores[5].start()
-    red_e.to_pair()
-    core = lax.rem(grp, 2)
-    stores.append(pltpu.make_async_copy(out_e.at[core], out_h.at[core], store_sem.at[6]))
-    stores[6].start()
     red_e.end()
     for copy in stores:
         copy.wait()
@@ -650,19 +641,18 @@
         ]
 
     return pl.pallas_call(
-        functools.partial(main_kernel, float((GR * NB * NG) ** -0.5)),
+        main_kernel,
         name="message_passing",
         out_shape=(
             jax.ShapeDtypeStruct((GR, L), BF16),
             jax.ShapeDtypeStruct((E, L), BF16),
             jax.ShapeDtypeStruct((E, L), F32),
             jax.ShapeDtypeStruct((GR, L), F32),
-            jax.ShapeDtypeStruct((2 * L, H), F32),
-            jax.ShapeDtypeStruct((H, L), F32),
+            jax.ShapeDtypeStruct((2, NB, 16 * NODE, L), BF16),
             jax.ShapeDtypeStruct((2, NB, 16 * EDGE, L), BF16),
         ),
         in_specs=anywhere(11),
-        out_specs=anywhere(7),
+        out_specs=anywhere(6),
         scratch_shapes=[
             vm((NB, 1, 128), jnp.int32),
             vm((E // 128, 1, 128), jnp.int32),
@@ -696,12 +686,10 @@
             vm((E, L), BF16),
             vm((NB, 128, L), BF16),
             vm((NB, 128, L), BF16),
-            vm((2 * L, H), F32),
-            vm((H, L), F32),
         ]
         + reduce_buffers(NODE)
         + reduce_buffers(EDGE)
-        + [sem((11,)), sem((7,))]
+        + [sem((11,)), sem((6,))]
         + [sem((NB,))] * 6
         + [sem((5,)), sem((5,)), sem((2, NB)), sem((2, NB))] * 2,
         compiler_params=pltpu.CompilerParams(
@@ -710,53 +698,52 @@
     )(*args)
 
 
-def finish_kernel(edge_scale, *refs):
-    count = 7
-    sources, targets = refs[:count], refs[count : 2 * count - 1]
-    g_ein_h, g_eout_h = refs[2 * count - 1 : 2 * count + 1]
-    held = refs[2 * count + 1 : 3 * count + 1]
-    g_ein, g_eout, load_sem, store_sem = refs[3 * count + 1 :]
-    loads = [
-        pltpu.make_async_copy(sources[i], held[i], load_sem.at[i]) for i in range(count)
-    ]
-    stores = [
-        pltpu.make_async_copy(held[i + 1], targets[i], store_sem.at[i]) for i in range(count - 1)
-    ]
-    stores += [
-        pltpu.make_async_copy(g_ein, g_ein_h, store_sem.at[count - 1]),
-        pltpu.make_async_copy(g_eout, g_eout_h, store_sem.at[count]),
-    ]
+def finish_kernel(edge_scale, node_scale, *refs):
+    sources, targets, results = refs[:6], refs[6:10], refs[10:14]
+    held, grads = refs[14:20], refs[20:24]
+    load_sem, store_sem = refs[24:]
+    loads = [pltpu.make_async_copy(sources[i], held[i], load_sem.at[i]) for i in range(6)]
+    stores = [pltpu.make_async_copy(held[i + 2], targets[i], store_sem.at[i]) for i in range(4)]
+    moves = [pltpu.make_async_copy(grads[i], results[i], store_sem.at[4 + i]) for i in range(4)]
     for copy in loads:
         copy.start()
-    out = held[0]
+    out_e, out_n = held[:2]
+    g_ein, g_eout, g_nin, g_nout = grads
     loads[0].wait()
     for b in range(3):
-        g_ein[128 * b : 128 * b + 128, :] = load_block(out, b, edge_scale)
-    stores[-2].start()
-    g_eout[...] = jnp.transpose(load_block(out, 3, edge_scale))
-    stores[-1].start()
-    for load, store in zip(loads[1:], stores):
+        g_ein[128 * b : 128 * b + 128, :] = load_block(out_e, b, edge_scale)
+    moves[0].start()
+    g_eout[...] = jnp.transpose(load_block(out_e, 3, edge_scale))
+    moves[1].start()
+    loads[1].wait()
+    for b in range(2):
+        g_nin[128 * b : 128 * b + 128, :] = load_block(out_n, b, node_scale)
+    moves[2].start()
+    g_nout[...] = jnp.transpose(load_block(out_n, 2, node_scale))
+    moves[3].start()
+    for load, store in zip(loads[2:], stores):
         load.wait()
         store.start()
-    for copy in stores:
+    for copy in moves + stores:
         copy.wait()
 
 
-def finish(out, *arrays):
-    grads = (
-        jax.ShapeDtypeStruct((3 * L, H), F32),
-        jax.ShapeDtypeStruct((H, L), F32),
+def finish(out_e, out_n, *arrays):
+    grads = tuple(
+        jax.ShapeDtypeStruct(shape, F32) for shape in ((3 * L, H), (H, L), (2 * L, H), (H, L))
     )
     return pl.pallas_call(
-        functools.partial(finish_kernel, float((E * NB * NG) ** -0.5)),
+        functools.partial(
+            finish_kernel, float((E * NB * NG) ** -0.5), float((GR * NB * NG) ** -0.5)
+        ),
         name="finish",
         out_shape=tuple(jax.ShapeDtypeStruct(a.shape, a.dtype) for a in arrays) + grads,
-        in_specs=anywhere(7),
+        in_specs=anywhere(6),
         out_specs=anywhere(8),
-        scratch_shapes=[pltpu.VMEM(a.shape, a.dtype) for a in (out,) + arrays + grads]
-        + [pltpu.SemaphoreType.DMA((7,)), pltpu.SemaphoreType.DMA((8,))],
+        scratch_shapes=[pltpu.VMEM(a.shape, a.dtype) for a in (out_e, out_n) + arrays + grads]
+        + [pltpu.SemaphoreType.DMA((6,)), pltpu.SemaphoreType.DMA((8,))],
         compiler_params=pltpu.CompilerParams(vmem_limit_bytes=VMEM_LIMIT),
-    )(out, *arrays)
+    )(out_e, out_n, *arrays)
 
 
 def on_device(
@@ -772,7 +759,7 @@
     node_cot,
     edge_cot,
 ):
-    *arrays, out = main(
+    *arrays, out_n, out_e = main(
         wanted_rows.reshape(NB, 1, 128),
         sender_slot.reshape(E // 128, 1, 128),
         receiver.reshape(E // 128, 1, 128),
@@ -785,7 +772,9 @@
         node_cot,
         edge_cot,
     )
-    new_nodes, new_edges, edge_grad, node_grad, g_nin, g_nout, g_ein, g_eout = finish(out, *arrays)
+    new_nodes, new_edges, edge_grad, node_grad, g_ein, g_eout, g_nin, g_nout = finish(
+        out_e, out_n, *arrays
+    )
     return new_nodes, new_edges, node_grad, edge_grad, g_ein, g_eout, g_nin, g_nout
 
 

time: 65.2 us -> 66.1 us (1.014)
  Pallas kernels: 64.3 us -> 65.2 us
    pallas_call x1, Pallas kernels: 60.1 us -> 61.1 us  [main(): pl.pallas_call(main_kernel, name='message_passing', out_shape=(jax.ShapeD...]
where the time goes in v2:
time: 66.1 us; the launch traced here: 66 us
  Pallas kernels  65.2 us (99%)
  between operations  0.81 us (1%)
    pallas_call x1, Pallas kernels, main(): pl.pallas_call(main_kernel, name='message_passing', out_shape=(jax.ShapeD...  61.1 us
    pallas_call x1, Pallas kernels, finish(): pl.pallas_call(functools.partial(finish_kernel, float((E * NB * NG) ** (-...  4.15 us

profile of v2, /device:TPU:1, one launch (start us, length us, event | category | flops | bytes accessed | tf_op | source)
XLA Modules:
  0.0 66.0 jit_solution(14191939891358300273)
XLA Ops:
  0.6 61.1 %message_passing.1 = (bf16[1024,128]{1,0:T(8,128)(2,1)}, bf16[4096,128]{1,0:T(8,128)(2,1)}, f32[4096,128]{1,0:T(8,128)}, f32[1024,128]{1,0:T(8,128)}, bf16[2,16,...) custom-call(s32[16,1,128]{2,1,0:T(1,128)} %bitcast.5, s32[32,1,128]{2,1,0:T(1,128)} %bitcast.3, ...), custom_call_target="tpu_custom_call" | custom-call | tf_op jit(solution)/shard_map/message_passing/pallas_call | solution.py:643
  61.7 4.1 %finish.1 = (bf16[1024,128]{1,0:T(8,128)(2,1)}, bf16[4096,128]{1,0:T(8,128)(2,1)}, f32[4096,128]{1,0:T(8,128)}, f32[1024,128]{1,0:T(8,128)}, f32[384,512]{1,0:T(...) custom-call(bf16[2,16,64,128]{3,2,1,0:T(8,128)(2,1)} %get-tuple-element.22.refs_0_, ...), custom_call_target="tpu_custom_call" | custom-call | tf_op jit(solution)/shard_map/finish/pallas_call | solution.py:735
